TPU v7x, 128 devices: a whole 4x4x4 slice. The times are simulated.
128 devices in a mesh: ctx: 16 (over y, z_hi, core), exp: 8 (over x, z_lo).
Axes of the slice: x: 4, y: 4, z: 4 (z_hi: 2, z_lo: 2; z = z_hi * 2 + z_lo), core: 2. Of those that a mesh axis runs over, the one named last changes fastest.
Arguments:
- span_q: bfloat16 [2048, 6144], P('ctx', 'exp'), may hold values from -9 to 9
- prompt_kv: bfloat16 [2, 16384, 1024], P(None, 'ctx', 'exp'), may hold values from -10 to 10
- span_kv: bfloat16 [2, 2048, 1024], P(None, 'ctx', 'exp'), may hold values from -10 to 10
- decode_q: bfloat16 [256, 6144], P('ctx', 'exp'), may hold values from -4 to 4
- decode_cache: bfloat16 [2, 256, 256, 1024], P(None, 'ctx', None, 'exp'), may hold values from -10 to 10
- decode_new: bfloat16 [2, 256, 1024], P(None, 'ctx', 'exp'), may hold values from -10.5 to 10.5
- decode_len: int32 [256], P('ctx'), may hold values from 1 to 256, as said below
- residual: bfloat16 [2304, 6144], P('ctx', 'exp'), may hold values from -1.5 to 1.5
- norm_gain: bfloat16 [6144], P('exp'), may hold values from 0.099609375 to 1.8984375
- router: bfloat16 [6144, 8], P('exp'), may hold values from -0.078125 to 0.078125
- expert_ids: int32 [2304, 2], P('ctx'), may hold values from 0 to 7, all different within a row; in each aligned block of 144 rows (0 to 143, 144 to 287, ...) at most 40 rows name the same one
- capacity: int32 [8], replicated, may hold values from 20 to 40, as said below
- w_gate: bfloat16 [8, 6144, 8192], P('exp', None, 'ctx'), may hold values from -0.078125 to 0.078125
- w_up: bfloat16 [8, 6144, 8192], P('exp', None, 'ctx'), may hold values from -0.078125 to 0.078125
- w_down: bfloat16 [8, 8192, 6144], P('exp', 'ctx'), may hold values from -0.0625 to 0.0625
Outputs:
- mixed: bfloat16 [2304, 6144], P('ctx', 'exp')
Inputs may be any that keep to these rules, and one draw needn't show every extreme that they name: `decode_len`: some decode row has exactly 256 cached positions. Some expert's capacity is exactly 40. `expert_ids`: in each row block of 144 rows (the rows of one ctx index) no expert is named by more than 40 rows; in some block some expert is named by exactly 40 rows.
All inputs are finite; a program needn't handle non-finite values.
Results may differ from a plain program's by a relative error of at most 0.019.
Values may be sent and summed in bfloat16 or wider, within the bound.
No kernel may reach another device: no remote copies, remote signals or barrier semaphores. Data moves between devices by JAX's collectives and lax.ppermute only.
A program may use at most 192 MiB of HBM per device.

v0:
```python
import jax
import jax.numpy as jnp
from jax import lax
from jax.sharding import PartitionSpec as P

D = 6144
HD = 128
QPK = 6
EXPERTS = 8
TOPK = 2
CAP = 40


NEG = -1e30
EPS = 1e-05


def from_behind(value, axis, steps):
    count = lax.axis_size(axis)
    pairs = [(source, (source + steps) % count) for source in range(count)]
    return lax.ppermute(value, axis, pairs)


def fold_block(state, queries, keys, values, visible):
    best, total, summed = state
    scores = jnp.einsum(
        "cgqd,kgd->gqck", queries, keys, preferred_element_type=jnp.float32
    ) * HD ** (-0.5)
    shown = visible[None, None, :, :]
    scores = jnp.where(shown, scores, NEG)
    newest = jnp.maximum(best, jnp.max(scores, axis=-1))
    factor = jnp.exp(best - newest)
    weights = jnp.where(shown, jnp.exp(scores - newest[..., None]), 0.0)
    total = total * factor + jnp.sum(weights, axis=-1)
    summed = summed * factor[..., None] + jnp.einsum(
        "gqck,kgd->gqcd", weights.astype(jnp.bfloat16), values, preferred_element_type=jnp.float32
    )
    return (newest, total, summed)


def decode_block(decode_q, decode_cache, decode_new, decode_len, groups):
    rows = decode_q.shape[0]
    length = decode_cache.shape[2]
    queries = decode_q.reshape(rows, groups, QPK, HD)
    keys = decode_cache[0].reshape(rows, length, groups, HD)
    values = decode_cache[1].reshape(rows, length, groups, HD)
    own_key = decode_new[0].reshape(rows, groups, HD)
    own_value = decode_new[1].reshape(rows, groups, HD)
    scale = HD ** (-0.5)
    scores = (
        jnp.einsum("rgqd,rlgd->rgql", queries, keys, preferred_element_type=jnp.float32) * scale
    )
    live = (jnp.arange(length, dtype=jnp.int32)[None, :] < decode_len[:, None])[:, None, None, :]
    own = jnp.einsum("rgqd,rgd->rgq", queries, own_key, preferred_element_type=jnp.float32) * scale
    top = jnp.maximum(jnp.max(jnp.where(live, scores, NEG), axis=-1), own)
    weights = jnp.where(live, jnp.exp(scores - top[..., None]), 0.0)
    own_weight = jnp.exp(own - top)
    own_prob = lax.optimization_barrier(own_weight.astype(jnp.bfloat16)).astype(jnp.float32)
    summed = jnp.einsum(
        "rgql,rlgd->rgqd", weights.astype(jnp.bfloat16), values, preferred_element_type=jnp.float32
    )
    summed = summed + own_prob[..., None] * own_value.astype(jnp.float32)[:, :, None, :]
    result = summed / (jnp.sum(weights, axis=-1) + own_weight)[..., None]
    return result.reshape(rows, groups * QPK * HD).astype(jnp.bfloat16)


def on_device(
    span_q,
    prompt_kv,
    span_kv,
    decode_q,
    decode_cache,
    decode_new,
    decode_len,
    residual,
    norm_gain,
    router,
    expert_ids,
    capacity,
    w_gate,
    w_up,
    w_down,
):
    groups = prompt_kv.shape[2] // HD
    span_rows = span_q.shape[0]
    prompt_rows = prompt_kv.shape[1]
    local_width = prompt_rows + span_rows
    loop_size = lax.axis_size("ctx")
    here = lax.axis_index("ctx")
    queries = span_q.reshape(span_rows, groups, QPK, HD)
    local_kv = jnp.concatenate([prompt_kv, span_kv], axis=1)
    keys = local_kv[0].reshape(local_width, groups, HD)
    values = local_kv[1].reshape(local_width, groups, HD)
    query_place = jnp.arange(span_rows, dtype=jnp.int32)
    key_place = jnp.arange(local_width, dtype=jnp.int32)
    empty = (
        jnp.full((groups, QPK, span_rows), NEG, jnp.float32),
        jnp.zeros((groups, QPK, span_rows), jnp.float32),
        jnp.zeros((groups, QPK, span_rows, HD), jnp.float32),
    )

    def visible_from(source):
        span_key = here * span_rows + key_place - prompt_rows
        span_query = source * span_rows + query_place
        return (key_place[None, :] < prompt_rows) | (span_key[None, :] <= span_query[:, None])

    def loop_step(step, carry):
        moving, best, total, summed = carry
        source = (here - step) % loop_size
        best, total, summed = fold_block(
            (best, total, summed), moving, keys, values, visible_from(source)
        )
        moving = from_behind(moving, "ctx", 1)
        best, total, summed = from_behind((best, total, summed), "ctx", 1)
        return (moving, best, total, summed)

    leftover, best, total, summed = lax.fori_loop(0, loop_size, loop_step, (queries,) + empty)
    span_out = (
        (summed / total[..., None])
        .transpose(2, 0, 1, 3)
        .reshape(span_rows, groups * QPK * HD)
        .astype(jnp.bfloat16)
    )
    decode_out = decode_block(decode_q, decode_cache, decode_new, decode_len, groups)
    attn = jnp.concatenate([span_out, decode_out], axis=0)
    carried = residual.astype(jnp.float32) + attn.astype(jnp.float32)
    gained = carried * norm_gain.astype(jnp.float32)
    squares = jnp.sum(carried * carried, axis=1)
    partial_logits = jnp.dot(gained, router.astype(jnp.float32), precision=lax.Precision.HIGHEST)
    squares, logits = lax.psum((squares, partial_logits), "exp")
    rscale = lax.rsqrt(squares / D + EPS)
    logits = logits * rscale[:, None]
    normed = (gained * rscale[:, None]).astype(jnp.bfloat16)
    row_count = expert_ids.shape[0]
    slots = CAP * EXPERTS
    expert_range = jnp.arange(EXPERTS, dtype=jnp.int32)
    onehot = expert_ids[:, :, None] == expert_range[None, None, :]
    chosen = jnp.sum(jnp.where(onehot, logits[:, None, :], 0.0), axis=-1)
    route_weight = jax.nn.sigmoid(chosen - chosen[:, ::-1])
    flat_ids = expert_ids.reshape(row_count * TOPK)
    assign = onehot.reshape(row_count * TOPK, EXPERTS).astype(jnp.int32)
    prior = jnp.cumsum(assign, axis=0) - assign
    position = jnp.sum(prior * assign, axis=1)
    limit = jnp.sum(assign * capacity[None, :], axis=1)
    kept = position < limit
    slot_index = position * EXPERTS + flat_ids
    select = kept[:, None] & (slot_index[:, None] == jnp.arange(slots, dtype=jnp.int32)[None, :])
    select = select.reshape(row_count, TOPK, slots)
    placing = jnp.sum(select.astype(jnp.float32), axis=1).astype(jnp.bfloat16)
    outgoing = jnp.einsum("rs,rd->sd", placing, normed, preferred_element_type=jnp.float32).astype(
        jnp.bfloat16
    )
    outgoing = outgoing.reshape(CAP, EXPERTS, normed.shape[1])
    arrived = lax.all_to_all(outgoing, "exp", split_axis=1, concat_axis=2, tiled=True)
    piece = lax.all_gather(arrived, "ctx", axis=0, tiled=True)
    gate = jnp.einsum("red,edf->ref", piece, w_gate, preferred_element_type=jnp.float32)
    up = jnp.einsum("red,edf->ref", piece, w_up, preferred_element_type=jnp.float32)
    hidden = (jax.nn.silu(gate) * up).astype(jnp.bfloat16)
    result = lax.psum_scatter(
        jnp.einsum("ref,efd->red", hidden, w_down, preferred_element_type=jnp.float32).astype(
            jnp.bfloat16
        ),
        "ctx",
        scatter_dimension=0,
        tiled=True,
    )
    returned = lax.all_to_all(result, "exp", split_axis=2, concat_axis=1, tiled=True)
    returned = returned.reshape(slots, returned.shape[2]).astype(jnp.float32)
    mixing = jnp.sum(select.astype(jnp.float32) * route_weight[:, :, None], axis=1)
    moe = jnp.dot(mixing, returned, precision=lax.Precision.HIGHEST)
    return (carried + moe).astype(jnp.bfloat16)


def solution(mesh):
    placed = (
        P("ctx", "exp"),
        P(None, "ctx", "exp"),
        P(None, "ctx", "exp"),
        P("ctx", "exp"),
        P(None, "ctx", None, "exp"),
        P(None, "ctx", "exp"),
        P("ctx"),
        P("ctx", "exp"),
        P("exp"),
        P("exp", None),
        P("ctx", None),
        P(),
        P("exp", None, "ctx"),
        P("exp", None, "ctx"),
        P("exp", "ctx", None),
    )
    return jax.shard_map(
        on_device, mesh=mesh, in_specs=placed, out_specs=P("ctx", "exp"), check_vma=False
    )
```

profile of v0, /device:TPU:0, one launch (start us, length us, event | category | flops | bytes accessed | tf_op | source)
XLA Modules:
  0.0 548.6 jit_solution(14432433886619522714)
XLA Ops:
  18.0 231.0 %while.23 = (s32[]{:T(128)}, bf16[128,1,6,128]{3,0,2,1:T(8,128)(2,1)S(1)}, f32[1,6,128]{2,1,0:T(8,128)S(1)}, f32[1,6,128]{2,1,0:T(8,128)S(1)}, f32[1,6,128,128]{...) while((s32[]{:T(128)}, ...), condition=%wide.region_3.4_spmd.clone.clone, body=%wide.region_0.3_spmd.clone.clone.sunk | while | flops 461444864 | bytes 15618738 | solution.py:117
  27.4 8.3 %collective-permute-done.2 = f32[1,6,128]{2,1,0:T(8,128)S(1)} collective-permute-done((f32[1,6,128]{2,1,0:T(8,128)S(1)}, f32[1,6,128]{2,1,0:T(8,128)S(1)}, u32[]{:S(2)}, u32[]{:S(2)}) %collective-permute-start.2) | collective-permute-done | bytes 3104 | tf_op jit(solution)/shard_map/while/body/eval_jaxpr/ppermute | solution.py:21
  58.2 6.1 %collective-permute-done.2 = f32[1,6,128]{2,1,0:T(8,128)S(1)} collective-permute-done((f32[1,6,128]{2,1,0:T(8,128)S(1)}, f32[1,6,128]{2,1,0:T(8,128)S(1)}, u32[]{:S(2)}, u32[]{:S(2)}) %collective-permute-start.2) | collective-permute-done | bytes 3104 | tf_op jit(solution)/shard_map/while/body/eval_jaxpr/ppermute | solution.py:21
  86.8 6.1 %collective-permute-done.2 = f32[1,6,128]{2,1,0:T(8,128)S(1)} collective-permute-done((f32[1,6,128]{2,1,0:T(8,128)S(1)}, f32[1,6,128]{2,1,0:T(8,128)S(1)}, u32[]{:S(2)}, u32[]{:S(2)}) %collective-permute-start.2) | collective-permute-done | bytes 3104 | tf_op jit(solution)/shard_map/while/body/eval_jaxpr/ppermute | solution.py:21
  115.5 5.8 %collective-permute-done.2 = f32[1,6,128]{2,1,0:T(8,128)S(1)} collective-permute-done((f32[1,6,128]{2,1,0:T(8,128)S(1)}, f32[1,6,128]{2,1,0:T(8,128)S(1)}, u32[]{:S(2)}, u32[]{:S(2)}) %collective-permute-start.2) | collective-permute-done | bytes 3104 | tf_op jit(solution)/shard_map/while/body/eval_jaxpr/ppermute | solution.py:21
  143.8 5.9 %collective-permute-done.2 = f32[1,6,128]{2,1,0:T(8,128)S(1)} collective-permute-done((f32[1,6,128]{2,1,0:T(8,128)S(1)}, f32[1,6,128]{2,1,0:T(8,128)S(1)}, u32[]{:S(2)}, u32[]{:S(2)}) %collective-permute-start.2) | collective-permute-done | bytes 3104 | tf_op jit(solution)/shard_map/while/body/eval_jaxpr/ppermute | solution.py:21
  172.2 6.1 %collective-permute-done.2 = f32[1,6,128]{2,1,0:T(8,128)S(1)} collective-permute-done((f32[1,6,128]{2,1,0:T(8,128)S(1)}, f32[1,6,128]{2,1,0:T(8,128)S(1)}, u32[]{:S(2)}, u32[]{:S(2)}) %collective-permute-start.2) | collective-permute-done | bytes 3104 | tf_op jit(solution)/shard_map/while/body/eval_jaxpr/ppermute | solution.py:21
  187.2 4.8 collective-permute-done.2
  200.9 6.1 %collective-permute-done.2 = f32[1,6,128]{2,1,0:T(8,128)S(1)} collective-permute-done((f32[1,6,128]{2,1,0:T(8,128)S(1)}, f32[1,6,128]{2,1,0:T(8,128)S(1)}, u32[]{:S(2)}, u32[]{:S(2)}) %collective-permute-start.2) | collective-permute-done | bytes 3104 | tf_op jit(solution)/shard_map/while/body/eval_jaxpr/ppermute | solution.py:21
  215.8 4.8 collective-permute-done.2
  229.5 5.8 %collective-permute-done.2 = f32[1,6,128]{2,1,0:T(8,128)S(1)} collective-permute-done((f32[1,6,128]{2,1,0:T(8,128)S(1)}, f32[1,6,128]{2,1,0:T(8,128)S(1)}, u32[]{:S(2)}, u32[]{:S(2)}) %collective-permute-start.2) | collective-permute-done | bytes 3104 | tf_op jit(solution)/shard_map/while/body/eval_jaxpr/ppermute | solution.py:21
  244.2 4.8 collective-permute-done.2
  249.9 19.8 %all-reduce.1 = (f32[144,8]{0,1:T(8,128)S(1)}, f32[144]{0:T(256)S(1)}) all-reduce(f32[144,8]{0,1:T(8,128)S(1)} %fusion.68, f32[144]{0:T(256)S(1)} %multiply_reduce_fusion), channel_id=1, replica_groups=mesh['ctx'=16,'exp'=8] {'exp'}, use_global_device_ids=true, to_apply=%region_10.11 | all-reduce | flops 1296 | bytes 10368 | tf_op jit(solution)/shard_map/psum | solution.py:130
  271.2 10.6 %all_to_all.21 = bf16[40,8,768]{2,0,1:T(8,128)(2,1)S(1)} all-to-all(bf16[40,8,768]{2,0,1:T(8,128)(2,1)S(1)} %copy.89), channel_id=1, replica_groups=mesh['ctx'=16,'exp'=8] {'exp'}, dimensions={1} | all-to-all | bytes 983040 | tf_op jit(solution)/shard_map/all_to_all | solution.py:154
  283.2 68.9 %all-gather.2.cloned.1.call-done = bf16[640,1,6144]{2,0,1:T(8,128)(2,1)} async-done(((bf16[40,1,6144]{2,0,1:T(8,128)(2,1)}), bf16[640,1,6144]{2,0,1:T(8,128)(2,1)}) %all-gather.2.cloned.1.call-update) | async-done | bytes 7864336 | tf_op jit(solution)/shard_map/all_gather | solution.py:155
  352.1 8.5 %fusion.34 = f32[640,1,512]{2,0,1:T(8,128)S(1)} fusion(bf16[1,6144,512]{2,1,0:T(8,128)(2,1)} %param.29, bf16[640,1,6144]{2,0,1:T(8,128)(2,1)} %all-gather.2.cloned.1.call-done), kind=kOutput, calls=%fused_computation.37 | convolution fusion | flops 4026531840 | bytes 15466496 | tf_op jit(solution)/shard_map/red,edf->ref/dot_general | solution.py:156
  360.7 7.3 %fusion.54 = bf16[640,512]{1,0:T(8,128)(2,1)S(1)} fusion(bf16[1,6144,512]{2,1,0:T(8,128)(2,1)} %param.30, bf16[640,1,6144]{2,0,1:T(8,128)(2,1)S(1)} %copy-done.6, f32[640,1,512]{2,0,1:T(8,128)S(1)} %fusion.34), kind=kOutput, calls=%fused_computation.42 | convolution fusion | flops 4028497920 | bytes 16121856 | tf_op jit(solution)/shard_map/red,edf->ref/dot_general | solution.py:157
  368.0 6.5 %fusion.26 = bf16[640,1,6144]{2,0,1:T(8,128)(2,1)} fusion(bf16[640,512]{1,0:T(8,128)(2,1)S(1)} %fusion.54, bf16[1,512,6144]{2,1,0:T(8,128)(2,1)S(1)} %bitcast.186), kind=kOutput, calls=%fused_computation.29 | convolution fusion | flops 4030464000 | bytes 14811136 | tf_op jit(solution)/shard_map/ref,efd->red/dot_general | solution.py:160
  374.5 94.7 %reduce-scatter.2.cloned.1.call-done = bf16[40,1,6144]{2,0,1:T(8,128)(2,1)} async-done(((bf16[640,1,6144]{2,0,1:T(8,128)(2,1)}), bf16[40,1,6144]{2,0,1:T(8,128)(2,1)}) %reduce-scatter.2.cloned.1.call-update) | async-done | bytes 491536 | tf_op jit(solution)/shard_map/reduce_scatter | solution.py:159
  469.2 6.2 %copy.91 = bf16[40,1,6144]{0,1,2:T(2,128)(2,1)S(1)} copy(bf16[40,1,6144]{2,0,1:T(8,128)(2,1)} %reduce-scatter.2.cloned.1.call-done) | data formatting | bytes 983040 | tf_op jit(solution)/shard_map/reduce_scatter | solution.py:159
  476.0 34.4 %reduce.18 = bf16[6144,40]{1,0:T(8,128)(2,1)} reduce(bf16[6144,1,40]{2,1,0:T(2,128)(2,1)S(1)} %bitcast.169, bf16[]{:T(256)} %broadcast.196), dimensions={1}, to_apply=%bitcast.135.reduce_sub_computation | reduce | bytes 983042
  514.5 12.6 %all_to_all.22 = bf16[8,2,15360]{2,1,0:T(2,128)(2,1)} all-to-all(bf16[8,2,15360]{2,1,0:T(2,128)(2,1)S(1)} %reshape.365), channel_id=1, replica_groups=mesh['ctx'=16,'exp'=8] {'exp'}, dimensions={0} | all-to-all | bytes 983040 | tf_op jit(solution)/shard_map/all_to_all | solution.py:167
  527.2 6.2 %reshape.366 = bf16[6144,1,40]{2,1,0:T(2,128)(2,1)S(1)} reshape(bf16[8,2,15360]{2,1,0:T(2,128)(2,1)} %all_to_all.22) | data formatting | bytes 983040
  533.4 4.9 copy.92
  (373 shorter events, 187.6 us)
Async XLA Ops:
  6.5 345.6 %all-gather.2.cloned.1.call-start = ((), (), s32[]{:S(2)}) async-start(), calls=%async_computation.3 | async-start | bytes 8355840 | tf_op jit(solution)/shard_map/all_gather | solution.py:155
  18.1 17.6 %collective-permute-start = (bf16[128,1,6,128]{3,0,2,1:T(8,128)(2,1)S(1)}, bf16[128,1,6,128]{3,0,2,1:T(8,128)(2,1)S(1)}, u32[]{:S(2)}, u32[]{:S(2)}) collective-permute-start(bf16[128,1,6,128]{3,0,2,1:T(8,128)(2,1)S(1)} %copy.108), channel_id=1, source_target_pairs={{0,8},{8,16},{16,24},{24,32},{32,40},{40,48},{48,56},{56,64},{64,7... | collective-permute-start | bytes 589832 | tf_op jit(solution)/shard_map/while/body/eval_jaxpr/ppermute | solution.py:21
  24.8 10.9 %collective-permute-start.3 = (f32[1,6,128,128]{3,2,1,0:T(8,128)S(1)}, f32[1,6,128,128]{3,2,1,0:T(8,128)S(1)}, u32[]{:S(2)}, u32[]{:S(2)}) collective-permute-start(f32[1,6,128,128]{3,2,1,0:T(8,128)S(1)} %fusion.108), channel_id=1, source_target_pairs={{0,8},{8,16},{16,24},{24,32},{32,40},{40,48},{48,56},{56,64},{64,7... | collective-permute-start | bytes 1179656 | tf_op jit(solution)/shard_map/while/body/eval_jaxpr/ppermute | solution.py:21
  35.7 13.6 %collective-permute-start = (bf16[128,1,6,128]{3,0,2,1:T(8,128)(2,1)S(1)}, bf16[128,1,6,128]{3,0,2,1:T(8,128)(2,1)S(1)}, u32[]{:S(2)}, u32[]{:S(2)}) collective-permute-start(bf16[128,1,6,128]{3,0,2,1:T(8,128)(2,1)S(1)} %copy.108), channel_id=1, source_target_pairs={{0,8},{8,16},{16,24},{24,32},{32,40},{40,48},{48,56},{56,64},{64,7... | collective-permute-start | bytes 589832 | tf_op jit(solution)/shard_map/while/body/eval_jaxpr/ppermute | solution.py:21
  38.4 10.9 %collective-permute-start.3 = (f32[1,6,128,128]{3,2,1,0:T(8,128)S(1)}, f32[1,6,128,128]{3,2,1,0:T(8,128)S(1)}, u32[]{:S(2)}, u32[]{:S(2)}) collective-permute-start(f32[1,6,128,128]{3,2,1,0:T(8,128)S(1)} %fusion.108), channel_id=1, source_target_pairs={{0,8},{8,16},{16,24},{24,32},{32,40},{40,48},{48,56},{56,64},{64,7... | collective-permute-start | bytes 1179656 | tf_op jit(solution)/shard_map/while/body/eval_jaxpr/ppermute | solution.py:21
  49.4 14.9 %collective-permute-start = (bf16[128,1,6,128]{3,0,2,1:T(8,128)(2,1)S(1)}, bf16[128,1,6,128]{3,0,2,1:T(8,128)(2,1)S(1)}, u32[]{:S(2)}, u32[]{:S(2)}) collective-permute-start(bf16[128,1,6,128]{3,0,2,1:T(8,128)(2,1)S(1)} %copy.108), channel_id=1, source_target_pairs={{0,8},{8,16},{16,24},{24,32},{32,40},{40,48},{48,56},{56,64},{64,7... | collective-permute-start | bytes 589832 | tf_op jit(solution)/shard_map/while/body/eval_jaxpr/ppermute | solution.py:21
  53.4 10.9 %collective-permute-start.3 = (f32[1,6,128,128]{3,2,1,0:T(8,128)S(1)}, f32[1,6,128,128]{3,2,1,0:T(8,128)S(1)}, u32[]{:S(2)}, u32[]{:S(2)}) collective-permute-start(f32[1,6,128,128]{3,2,1,0:T(8,128)S(1)} %fusion.108), channel_id=1, source_target_pairs={{0,8},{8,16},{16,24},{24,32},{32,40},{40,48},{48,56},{56,64},{64,7... | collective-permute-start | bytes 1179656 | tf_op jit(solution)/shard_map/while/body/eval_jaxpr/ppermute | solution.py:21
  64.4 13.6 %collective-permute-start = (bf16[128,1,6,128]{3,0,2,1:T(8,128)(2,1)S(1)}, bf16[128,1,6,128]{3,0,2,1:T(8,128)(2,1)S(1)}, u32[]{:S(2)}, u32[]{:S(2)}) collective-permute-start(bf16[128,1,6,128]{3,0,2,1:T(8,128)(2,1)S(1)} %copy.108), channel_id=1, source_target_pairs={{0,8},{8,16},{16,24},{24,32},{32,40},{40,48},{48,56},{56,64},{64,7... | collective-permute-start | bytes 589832 | tf_op jit(solution)/shard_map/while/body/eval_jaxpr/ppermute | solution.py:21
  78.0 14.9 %collective-permute-start = (bf16[128,1,6,128]{3,0,2,1:T(8,128)(2,1)S(1)}, bf16[128,1,6,128]{3,0,2,1:T(8,128)(2,1)S(1)}, u32[]{:S(2)}, u32[]{:S(2)}) collective-permute-start(bf16[128,1,6,128]{3,0,2,1:T(8,128)(2,1)S(1)} %copy.108), channel_id=1, source_target_pairs={{0,8},{8,16},{16,24},{24,32},{32,40},{40,48},{48,56},{56,64},{64,7... | collective-permute-start | bytes 589832 | tf_op jit(solution)/shard_map/while/body/eval_jaxpr/ppermute | solution.py:21
  82.0 10.9 %collective-permute-start.3 = (f32[1,6,128,128]{3,2,1,0:T(8,128)S(1)}, f32[1,6,128,128]{3,2,1,0:T(8,128)S(1)}, u32[]{:S(2)}, u32[]{:S(2)}) collective-permute-start(f32[1,6,128,128]{3,2,1,0:T(8,128)S(1)} %fusion.108), channel_id=1, source_target_pairs={{0,8},{8,16},{16,24},{24,32},{32,40},{40,48},{48,56},{56,64},{64,7... | collective-permute-start | bytes 1179656 | tf_op jit(solution)/shard_map/while/body/eval_jaxpr/ppermute | solution.py:21
  93.0 13.6 %collective-permute-start = (bf16[128,1,6,128]{3,0,2,1:T(8,128)(2,1)S(1)}, bf16[128,1,6,128]{3,0,2,1:T(8,128)(2,1)S(1)}, u32[]{:S(2)}, u32[]{:S(2)}) collective-permute-start(bf16[128,1,6,128]{3,0,2,1:T(8,128)(2,1)S(1)} %copy.108), channel_id=1, source_target_pairs={{0,8},{8,16},{16,24},{24,32},{32,40},{40,48},{48,56},{56,64},{64,7... | collective-permute-start | bytes 589832 | tf_op jit(solution)/shard_map/while/body/eval_jaxpr/ppermute | solution.py:21
  95.7 10.9 %collective-permute-start.3 = (f32[1,6,128,128]{3,2,1,0:T(8,128)S(1)}, f32[1,6,128,128]{3,2,1,0:T(8,128)S(1)}, u32[]{:S(2)}, u32[]{:S(2)}) collective-permute-start(f32[1,6,128,128]{3,2,1,0:T(8,128)S(1)} %fusion.108), channel_id=1, source_target_pairs={{0,8},{8,16},{16,24},{24,32},{32,40},{40,48},{48,56},{56,64},{64,7... | collective-permute-start | bytes 1179656 | tf_op jit(solution)/shard_map/while/body/eval_jaxpr/ppermute | solution.py:21
  106.6 14.6 %collective-permute-start = (bf16[128,1,6,128]{3,0,2,1:T(8,128)(2,1)S(1)}, bf16[128,1,6,128]{3,0,2,1:T(8,128)(2,1)S(1)}, u32[]{:S(2)}, u32[]{:S(2)}) collective-permute-start(bf16[128,1,6,128]{3,0,2,1:T(8,128)(2,1)S(1)} %copy.108), channel_id=1, source_target_pairs={{0,8},{8,16},{16,24},{24,32},{32,40},{40,48},{48,56},{56,64},{64,7... | collective-permute-start | bytes 589832 | tf_op jit(solution)/shard_map/while/body/eval_jaxpr/ppermute | solution.py:21
  110.3 10.9 %collective-permute-start.3 = (f32[1,6,128,128]{3,2,1,0:T(8,128)S(1)}, f32[1,6,128,128]{3,2,1,0:T(8,128)S(1)}, u32[]{:S(2)}, u32[]{:S(2)}) collective-permute-start(f32[1,6,128,128]{3,2,1,0:T(8,128)S(1)} %fusion.108), channel_id=1, source_target_pairs={{0,8},{8,16},{16,24},{24,32},{32,40},{40,48},{48,56},{56,64},{64,7... | collective-permute-start | bytes 1179656 | tf_op jit(solution)/shard_map/while/body/eval_jaxpr/ppermute | solution.py:21
  121.3 13.6 %collective-permute-start = (bf16[128,1,6,128]{3,0,2,1:T(8,128)(2,1)S(1)}, bf16[128,1,6,128]{3,0,2,1:T(8,128)(2,1)S(1)}, u32[]{:S(2)}, u32[]{:S(2)}) collective-permute-start(bf16[128,1,6,128]{3,0,2,1:T(8,128)(2,1)S(1)} %copy.108), channel_id=1, source_target_pairs={{0,8},{8,16},{16,24},{24,32},{32,40},{40,48},{48,56},{56,64},{64,7... | collective-permute-start | bytes 589832 | tf_op jit(solution)/shard_map/while/body/eval_jaxpr/ppermute | solution.py:21
  135.0 14.8 %collective-permute-start = (bf16[128,1,6,128]{3,0,2,1:T(8,128)(2,1)S(1)}, bf16[128,1,6,128]{3,0,2,1:T(8,128)(2,1)S(1)}, u32[]{:S(2)}, u32[]{:S(2)}) collective-permute-start(bf16[128,1,6,128]{3,0,2,1:T(8,128)(2,1)S(1)} %copy.108), channel_id=1, source_target_pairs={{0,8},{8,16},{16,24},{24,32},{32,40},{40,48},{48,56},{56,64},{64,7... | collective-permute-start | bytes 589832 | tf_op jit(solution)/shard_map/while/body/eval_jaxpr/ppermute | solution.py:21
  149.8 13.6 %collective-permute-start = (bf16[128,1,6,128]{3,0,2,1:T(8,128)(2,1)S(1)}, bf16[128,1,6,128]{3,0,2,1:T(8,128)(2,1)S(1)}, u32[]{:S(2)}, u32[]{:S(2)}) collective-permute-start(bf16[128,1,6,128]{3,0,2,1:T(8,128)(2,1)S(1)} %copy.108), channel_id=1, source_target_pairs={{0,8},{8,16},{16,24},{24,32},{32,40},{40,48},{48,56},{56,64},{64,7... | collective-permute-start | bytes 589832 | tf_op jit(solution)/shard_map/while/body/eval_jaxpr/ppermute | solution.py:21
  163.4 14.9 %collective-permute-start = (bf16[128,1,6,128]{3,0,2,1:T(8,128)(2,1)S(1)}, bf16[128,1,6,128]{3,0,2,1:T(8,128)(2,1)S(1)}, u32[]{:S(2)}, u32[]{:S(2)}) collective-permute-start(bf16[128,1,6,128]{3,0,2,1:T(8,128)(2,1)S(1)} %copy.108), channel_id=1, source_target_pairs={{0,8},{8,16},{16,24},{24,32},{32,40},{40,48},{48,56},{56,64},{64,7... | collective-permute-start | bytes 589832 | tf_op jit(solution)/shard_map/while/body/eval_jaxpr/ppermute | solution.py:21
  178.4 13.7 %collective-permute-start = (bf16[128,1,6,128]{3,0,2,1:T(8,128)(2,1)S(1)}, bf16[128,1,6,128]{3,0,2,1:T(8,128)(2,1)S(1)}, u32[]{:S(2)}, u32[]{:S(2)}) collective-permute-start(bf16[128,1,6,128]{3,0,2,1:T(8,128)(2,1)S(1)} %copy.108), channel_id=1, source_target_pairs={{0,8},{8,16},{16,24},{24,32},{32,40},{40,48},{48,56},{56,64},{64,7... | collective-permute-start | bytes 589832 | tf_op jit(solution)/shard_map/while/body/eval_jaxpr/ppermute | solution.py:21
  192.1 14.9 %collective-permute-start = (bf16[128,1,6,128]{3,0,2,1:T(8,128)(2,1)S(1)}, bf16[128,1,6,128]{3,0,2,1:T(8,128)(2,1)S(1)}, u32[]{:S(2)}, u32[]{:S(2)}) collective-permute-start(bf16[128,1,6,128]{3,0,2,1:T(8,128)(2,1)S(1)} %copy.108), channel_id=1, source_target_pairs={{0,8},{8,16},{16,24},{24,32},{32,40},{40,48},{48,56},{56,64},{64,7... | collective-permute-start | bytes 589832 | tf_op jit(solution)/shard_map/while/body/eval_jaxpr/ppermute | solution.py:21
  207.0 13.7 %collective-permute-start = (bf16[128,1,6,128]{3,0,2,1:T(8,128)(2,1)S(1)}, bf16[128,1,6,128]{3,0,2,1:T(8,128)(2,1)S(1)}, u32[]{:S(2)}, u32[]{:S(2)}) collective-permute-start(bf16[128,1,6,128]{3,0,2,1:T(8,128)(2,1)S(1)} %copy.108), channel_id=1, source_target_pairs={{0,8},{8,16},{16,24},{24,32},{32,40},{40,48},{48,56},{56,64},{64,7... | collective-permute-start | bytes 589832 | tf_op jit(solution)/shard_map/while/body/eval_jaxpr/ppermute | solution.py:21
  220.7 14.6 %collective-permute-start = (bf16[128,1,6,128]{3,0,2,1:T(8,128)(2,1)S(1)}, bf16[128,1,6,128]{3,0,2,1:T(8,128)(2,1)S(1)}, u32[]{:S(2)}, u32[]{:S(2)}) collective-permute-start(bf16[128,1,6,128]{3,0,2,1:T(8,128)(2,1)S(1)} %copy.108), channel_id=1, source_target_pairs={{0,8},{8,16},{16,24},{24,32},{32,40},{40,48},{48,56},{56,64},{64,7... | collective-permute-start | bytes 589832 | tf_op jit(solution)/shard_map/while/body/eval_jaxpr/ppermute | solution.py:21
  235.3 13.7 %collective-permute-start = (bf16[128,1,6,128]{3,0,2,1:T(8,128)(2,1)S(1)}, bf16[128,1,6,128]{3,0,2,1:T(8,128)(2,1)S(1)}, u32[]{:S(2)}, u32[]{:S(2)}) collective-permute-start(bf16[128,1,6,128]{3,0,2,1:T(8,128)(2,1)S(1)} %copy.108), channel_id=1, source_target_pairs={{0,8},{8,16},{16,24},{24,32},{32,40},{40,48},{48,56},{56,64},{64,7... | collective-permute-start | bytes 589832 | tf_op jit(solution)/shard_map/while/body/eval_jaxpr/ppermute | solution.py:21
  282.9 186.3 %reduce-scatter.2.cloned.1.call-start = ((), (), s32[]{:S(2)}) async-start(), calls=%async_computation.4 | async-start | bytes 8355840 | tf_op jit(solution)/shard_map/reduce_scatter | solution.py:159
  (51 other events, 1177.2 us)
Sparse Core Ops, SparseCore 0:
  283.1 69.0 all-gather.1
  374.6 94.5 reduce-scatter.1
where the time goes:
time: 550 us; the launch traced here: 549 us
  waiting for transfers between devices  287 us (52%)
  other arithmetic  65 us (12%)
  starting transfers between devices  56.7 us (10%)
  matrix products  53.6 us (10%)
  blocking collectives  43 us (8%)
  local copies, waits for them, and re-layouts  28.2 us (5%)
  between operations  13.8 us (3%)
    ppermute x64, waiting for transfers between devices, from_behind(): return lax.ppermute(value, axis, pairs)  123 us
    reduce_scatter x1, waiting for transfers between devices, on_device(): lax.psum_scatter(jnp.einsum('ref,efd->red', hidden, w_down, preferred_ele...  94.7 us
    all_gather x1, waiting for transfers between devices, on_device(): piece = lax.all_gather(arrived, 'ctx', axis=0, tiled=True)  68.9 us
    ppermute x64, starting transfers between devices, from_behind(): return lax.ppermute(value, axis, pairs)  56.4 us
    unnamed x2, other arithmetic  34.4 us
    psum x1, blocking collectives, on_device(): squares, logits = lax.psum((squares, partial_logits), 'exp')  19.8 us
    dot_general x16, matrix products, fold_block(): jnp.einsum('gqck,kgd->gqcd', weights.astype(jnp.bfloat16), values, prefer...  14.2 us
    or x16, other arithmetic, visible_from(): (key_place[None, :] < prompt_rows) | (span_key[None, :] <= span_query[:,...  14 us
  transfers between devices with their start and end apart: 66, of which 34 were waited for; matrix products, arithmetic and copies ran while one was open for 9% of the time, Pallas kernels for 0%

commit v1 on v0

v1 whole, which is shorter than its diff:
```python
import functools

import jax
import jax.numpy as jnp
from jax import lax
from jax.experimental import pallas as pl
from jax.experimental.pallas import tpu as pltpu
from jax.sharding import PartitionSpec as P

D = 6144
HD = 128
QPK = 6
EXPERTS = 8
TOPK = 2
CAP = 40
FF_DEV = 512
SPAN_DEV = 128
ROWS_DEV = 144
N_Y = 4
WIDTH = D // EXPERTS
SLOTS = CAP * EXPERTS
MSG = QPK * HD + 128
EXTRA = 8

F1 = 4096
F2 = D - F1

NEG = -1e30
EPS = 1e-05
LOG2E = 1.4426950408889634
SCALE2 = HD ** (-0.5) * LOG2E
BF16 = jnp.bfloat16
F32 = jnp.float32
MIB = 2**20
VMEM = pl.BlockSpec(memory_space=pltpu.VMEM)
SMEM = pl.BlockSpec(memory_space=pltpu.SMEM)


def ctx_index(y, z, core):
    return y * 4 + z * 2 + core


def moved(value, place):
    pairs = []
    for y in range(N_Y):
        for z in range(2):
            for core in range(2):
                pairs.append((ctx_index(y, z, core), ctx_index(*place(y, z, core))))
    return lax.ppermute(value, "ctx", pairs)


def along_y(value, steps):
    return moved(value, lambda y, z, core: ((y + steps) % N_Y, z, core))


def across_z(value):
    return moved(value, lambda y, z, core: (y, 1 - z, core))


def across_core(value):
    return moved(value, lambda y, z, core: (y, z, 1 - core))


def dot_nt(a, b, precision=None):
    return lax.dot_general(
        a, b, (((1,), (1,)), ((), ())), preferred_element_type=F32, precision=precision
    )


def head_weights(query, keys, span_keys, place, h):
    scores = dot_nt(query, keys)
    span = dot_nt(query, span_keys)
    row = lax.broadcasted_iota(jnp.int32, span.shape, 0) + place[0] * SPAN_DEV
    col = lax.broadcasted_iota(jnp.int32, span.shape, 1)
    where = jnp.where(
        col < SPAN_DEV, place[1] * SPAN_DEV + col, (place[2] - 1) * SPAN_DEV + col
    )
    span = jnp.where(where <= row, span, NEG)
    top = jnp.maximum(
        jnp.max(scores, axis=1, keepdims=True), jnp.max(span, axis=1, keepdims=True)
    )
    return (
        top,
        jnp.exp2((scores - top) * SCALE2).astype(BF16),
        jnp.exp2((span - top) * SCALE2).astype(BF16),
    )


def read_blocks(a_ref, b_ref):
    span = SPAN_DEV
    prompt = a_ref.shape[1] - span
    keys = jnp.concatenate([a_ref[0, :prompt, :], b_ref[0, :prompt, :]], axis=0)
    span_keys = jnp.concatenate([a_ref[0, prompt:, :], b_ref[0, prompt:, :]], axis=0)
    values = jnp.concatenate([a_ref[1, :prompt, :], b_ref[1, :prompt, :]], axis=0)
    span_values = jnp.concatenate([a_ref[1, prompt:, :], b_ref[1, prompt:, :]], axis=0)
    values = jnp.concatenate([values, jnp.ones(values.shape, BF16)], axis=1)
    span_values = jnp.concatenate([span_values, jnp.ones(span_values.shape, BF16)], axis=1)
    return keys, span_keys, values, span_values


def flash_first(place_ref, q_ref, a_ref, b_ref, sum_ref, total_ref, top_ref):
    keys, span_keys, values, span_values = read_blocks(a_ref, b_ref)
    place = (place_ref[0], place_ref[1], place_ref[2])
    for h in range(QPK):
        lanes = slice(h * HD, (h + 1) * HD)
        top, probs, span_probs = head_weights(q_ref[:, lanes], keys, span_keys, place, h)
        out = jnp.dot(probs, values, preferred_element_type=F32)
        out = out + jnp.dot(span_probs, span_values, preferred_element_type=F32)
        sum_ref[:, lanes] = out[:, :HD]
        total_ref[:, lanes] = out[:, HD:]
        top_ref[:, lanes] = jnp.broadcast_to(top, (SPAN_DEV, HD))


def split3(value):
    hi = value.astype(BF16).astype(F32)
    rest = value - hi
    mid = rest.astype(BF16).astype(F32)
    return hi, mid, rest - mid


def flash_last(place_ref, q_ref, a_ref, b_ref, sum_ref, total_ref, top_ref, msg_ref):
    keys, span_keys, values, span_values = read_blocks(a_ref, b_ref)
    place = (place_ref[0], place_ref[1], place_ref[2])
    lane = lax.broadcasted_iota(jnp.int32, (SPAN_DEV, 128), 1)
    stats = jnp.zeros((SPAN_DEV, 128), F32)
    for h in range(QPK):
        lanes = slice(h * HD, (h + 1) * HD)
        top, probs, span_probs = head_weights(q_ref[:, lanes], keys, span_keys, place, h)
        out = jnp.dot(probs, values, preferred_element_type=F32)
        out = out + jnp.dot(span_probs, span_values, preferred_element_type=F32)
        before = top_ref[:, lanes]
        newest = jnp.maximum(before, top)
        old = jnp.exp2((before - newest) * SCALE2)
        new = jnp.exp2((top - newest) * SCALE2)
        total = total_ref[:, lanes] * old + out[:, HD:] * new
        summed = sum_ref[:, lanes] * old + out[:, :HD] * new
        msg_ref[:, lanes] = (summed / total).astype(BF16)
        for i, part in enumerate(split3(newest * SCALE2 + jnp.log2(total))):
            stats = jnp.where(lane == 3 * h + i, part, stats)
    msg_ref[:, QPK * HD :] = stats.astype(BF16)


FLASH_COST = pl.CostEstimate(
    flops=4 * 768 * 2304 * 128, bytes_accessed=4 * MIB, transcendentals=768 * 2304
)


def flash_start(place, queries, block_a, block_b):
    shape = jax.ShapeDtypeStruct((SPAN_DEV, QPK * HD), F32)
    return pl.pallas_call(
        flash_first,
        out_shape=(shape,) * 3,
        in_specs=[SMEM, VMEM, VMEM, VMEM],
        out_specs=(VMEM,) * 3,
        compiler_params=pltpu.CompilerParams(vmem_limit_bytes=32 * MIB),
        cost_estimate=FLASH_COST,
        name="flash_first",
    )(place, queries, block_a, block_b)


def flash_end(place, queries, block_a, block_b, state):
    return pl.pallas_call(
        flash_last,
        out_shape=jax.ShapeDtypeStruct((SPAN_DEV, MSG), BF16),
        in_specs=[SMEM] + [VMEM] * 6,
        out_specs=VMEM,
        compiler_params=pltpu.CompilerParams(vmem_limit_bytes=32 * MIB),
        cost_estimate=FLASH_COST,
        name="flash_last",
    )(place, queries, block_a, block_b, *state)


def dispatch_kernel(
    m0, m1, m2, m3, decode_ref, residual_ref, gain_ref, router_ref, placing_ref, carried_ref, out_ref
):
    msgs = (m0, m1, m2, m3)
    for h in range(QPK):
        lanes = slice(h * HD, (h + 1) * HD)
        levels = []
        for m in msgs:
            at = QPK * HD + 3 * h
            stat = m[:, at : at + 3].astype(F32)
            levels.append(stat[:, 0:1] + stat[:, 1:2] + stat[:, 2:3])
        top = functools.reduce(jnp.maximum, levels)
        weights = [jnp.exp2(level - top) for level in levels]
        total = sum(weights)
        summed = sum(w * m[:, lanes].astype(F32) for w, m in zip(weights, msgs))
        attn = (summed / total).astype(BF16).astype(F32)
        carried_ref[:SPAN_DEV, lanes] = residual_ref[:SPAN_DEV, lanes].astype(F32) + attn
    carried_ref[SPAN_DEV:, :] = residual_ref[SPAN_DEV:, :].astype(F32) + decode_ref[...].astype(F32)
    carried = carried_ref[...]
    gained = carried * gain_ref[...].astype(F32)
    logits = dot_nt(router_ref[...].astype(F32), gained, lax.Precision.HIGHEST)
    squares = dot_nt(jnp.ones((EXTRA, WIDTH), F32), carried * carried, lax.Precision.HIGHEST)
    log_hi, log_mid, _ = split3(logits)
    sq_hi, sq_mid, _ = split3(squares)
    row = lax.broadcasted_iota(jnp.int32, squares.shape, 0)
    sq = jnp.where(row == 0, sq_hi, sq_mid)
    placed = jnp.dot(placing_ref[...], gained.astype(BF16), preferred_element_type=F32).astype(BF16)
    for e in range(EXPERTS):
        out_ref[e, :CAP, :] = placed[e * CAP : (e + 1) * CAP, :]
        out_ref[e, CAP:, :] = jnp.zeros((EXTRA, WIDTH), BF16)
        out_ref[e, CAP:, 0:ROWS_DEV] = log_hi.astype(BF16)
        out_ref[e, CAP:, 256 : 256 + ROWS_DEV] = log_mid.astype(BF16)
        out_ref[e, CAP:, 512 : 512 + ROWS_DEV] = sq.astype(BF16)


def arrive_kernel(got_ref, placing_ref, first_ref, second_ref, logits_ref):
    stats = got_ref[0, CAP:, :].astype(F32)
    for e in range(1, EXPERTS):
        stats = stats + got_ref[e, CAP:, :].astype(F32)
    logits = stats[:, 0:ROWS_DEV] + stats[:, 256 : 256 + ROWS_DEV]
    squares = stats[0:1, 512 : 512 + ROWS_DEV] + stats[1:2, 512 : 512 + ROWS_DEV]
    rscale = lax.rsqrt(squares / D + EPS)
    logits_ref[...] = logits * rscale
    scale = jnp.sum(placing_ref[...].astype(F32) * rscale, axis=1, keepdims=True)
    for e in range(EXPERTS):
        rows = (got_ref[e, :CAP, :].astype(F32) * scale).astype(BF16)
        begin = e * WIDTH
        end = begin + WIDTH
        if end <= F1:
            first_ref[:, begin:end] = rows
        elif begin >= F1:
            second_ref[:, begin - F1 : end - F1] = rows
        else:
            first_ref[:, begin:F1] = rows[:, : F1 - begin]
            second_ref[:, : end - F1] = rows[:, F1 - begin :]


def expert_inputs(pieces, x_ref):
    for ref, row, col in pieces:
        rows, cols = ref.shape
        x_ref[row : row + rows, col : col + cols] = ref[...]


def gate_first(layout, n_pieces, *refs):
    pieces = refs[:n_pieces]
    g_own, g_other, u_own, u_other, gate_ref, up_ref, x_ref = refs[n_pieces:]
    step = pl.program_id(0)

    @pl.when(step == 0)
    def _():
        expert_inputs([(r, *at) for r, at in zip(pieces, layout)], x_ref)

    @pl.when(step < 2)
    def _():
        gate_ref[...] = jnp.dot(x_ref[...], g_own[0], preferred_element_type=F32)
        up_ref[...] = jnp.dot(x_ref[...], u_own[0], preferred_element_type=F32)

    @pl.when(step >= 2)
    def _():
        gate_ref[...] = jnp.dot(x_ref[...], g_other[0], preferred_element_type=F32)
        up_ref[...] = jnp.dot(x_ref[...], u_other[0], preferred_element_type=F32)


def gate_last(layout, n_pieces, *refs):
    pieces = refs[:n_pieces]
    gate_ref, up_ref, g_own, g_other, u_own, u_other, hidden_ref, x_ref = refs[n_pieces:]
    step = pl.program_id(0)

    @pl.when(step == 0)
    def _():
        expert_inputs([(r, *at) for r, at in zip(pieces, layout)], x_ref)

    def finish(g, u):
        gate = gate_ref[...] + jnp.dot(x_ref[...], g, preferred_element_type=F32)
        up = up_ref[...] + jnp.dot(x_ref[...], u, preferred_element_type=F32)
        hidden_ref[...] = (gate / (1.0 + jnp.exp(-gate)) * up).astype(BF16)

    @pl.when(step < 2)
    def _():
        finish(g_own[0], u_own[0])

    @pl.when(step >= 2)
    def _():
        finish(g_other[0], u_other[0])


N_TILE = 256


def gate_specs(first, depth):
    own = pl.BlockSpec((1, depth, N_TILE), lambda n: (0, first, jnp.minimum(n, 1)))
    other = pl.BlockSpec((1, depth, N_TILE), lambda n: (0, first, jnp.maximum(n - 2, 0)))
    return [own, other, own, other]


def gate_call(kernel, pieces, layout, state, weights, first, depth, outs, dtype):
    whole = [pl.BlockSpec(p.shape, lambda n: (0, 0)) for p in pieces]
    tile = pl.BlockSpec((SLOTS, N_TILE), lambda n: (0, n))
    shape = jax.ShapeDtypeStruct((SLOTS, 2 * FF_DEV), dtype)
    return pl.pallas_call(
        functools.partial(kernel, layout, len(pieces)),
        grid=(2 * FF_DEV // N_TILE,),
        out_shape=(shape,) * outs,
        in_specs=whole + [tile] * len(state) + gate_specs(first, depth),
        out_specs=(tile,) * outs,
        scratch_shapes=[pltpu.VMEM((SLOTS, depth), BF16)],
        compiler_params=pltpu.CompilerParams(vmem_limit_bytes=48 * MIB),
        cost_estimate=pl.CostEstimate(
            flops=2 * SLOTS * depth * 4 * FF_DEV,
            bytes_accessed=depth * 4 * FF_DEV * 2,
            transcendentals=0,
        ),
        name=kernel.__name__,
    )(*pieces, *state, *weights)


def down_kernel(hidden_ref, own_ref, other_ref, out_ref):
    out = jnp.dot(hidden_ref[:, :FF_DEV], own_ref[0], preferred_element_type=F32)
    out = out + jnp.dot(hidden_ref[:, FF_DEV:], other_ref[0], preferred_element_type=F32)
    out_ref[...] = out.astype(BF16)


def down_call(hidden, own, other, first, width, tile):
    count = width // tile
    begin = first // tile
    weight = pl.BlockSpec((1, FF_DEV, tile), lambda n: (0, 0, begin + n))
    return pl.pallas_call(
        down_kernel,
        grid=(count,),
        out_shape=jax.ShapeDtypeStruct((SLOTS, width), BF16),
        in_specs=[pl.BlockSpec(hidden.shape, lambda n: (0, 0)), weight, weight],
        out_specs=pl.BlockSpec((SLOTS, tile), lambda n: (0, n)),
        compiler_params=pltpu.CompilerParams(vmem_limit_bytes=40 * MIB),
        cost_estimate=pl.CostEstimate(
            flops=2 * SLOTS * width * 2 * FF_DEV,
            bytes_accessed=width * 2 * FF_DEV * 2,
            transcendentals=0,
        ),
        name="down",
    )(hidden, own, other)


def final_kernel(hi_ref, lo_ref, got_ref, carried_ref, out_ref):
    got = got_ref[...]
    moe = jnp.dot(hi_ref[...], got, preferred_element_type=F32)
    moe = moe + jnp.dot(lo_ref[...], got, preferred_element_type=F32)
    out_ref[...] = (carried_ref[...] + moe).astype(BF16)


def mixing_kernel(slot_ref, weight_ref, hi_ref, lo_ref):
    lane = lax.broadcasted_iota(jnp.int32, (ROWS_DEV, SLOTS), 1)
    mix = jnp.zeros((ROWS_DEV, SLOTS), F32)
    for k in range(TOPK):
        mix = jnp.where(slot_ref[:, k : k + 1] == lane, weight_ref[:, k : k + 1], mix)
    hi = mix.astype(BF16)
    hi_ref[...] = hi
    lo_ref[...] = (mix - hi.astype(F32)).astype(BF16)


def decode_block(decode_q, decode_cache, decode_new, decode_len):
    rows = decode_q.shape[0]
    length = decode_cache.shape[2]
    queries = decode_q.reshape(rows, QPK, HD)
    keys = decode_cache[0]
    values = decode_cache[1]
    own_key = decode_new[0]
    own_value = decode_new[1]
    scale = HD ** (-0.5)
    scores = jnp.einsum("rqd,rld->rql", queries, keys, preferred_element_type=F32) * scale
    live = (jnp.arange(length, dtype=jnp.int32)[None, :] < decode_len[:, None])[:, None, :]
    own = jnp.einsum("rqd,rd->rq", queries, own_key, preferred_element_type=F32) * scale
    top = jnp.maximum(jnp.max(jnp.where(live, scores, NEG), axis=-1), own)
    weights = jnp.where(live, jnp.exp(scores - top[..., None]), 0.0)
    own_weight = jnp.exp(own - top)
    own_prob = lax.optimization_barrier(own_weight.astype(BF16)).astype(F32)
    summed = jnp.einsum("rql,rld->rqd", weights.astype(BF16), values, preferred_element_type=F32)
    summed = summed + own_prob[..., None] * own_value.astype(F32)[:, None, :]
    result = summed / (jnp.sum(weights, axis=-1) + own_weight)[..., None]
    return result.reshape(rows, QPK * HD).astype(BF16)


def add(*values):
    return functools.reduce(jnp.add, [v.astype(F32) for v in values]).astype(BF16)


def scatter_y(own, left, right, far):
    half = far.shape[1] // 2
    from_left = along_y(far[:, :half], 1)
    from_right = along_y(far[:, half:], -1)
    right = jnp.concatenate([add(right[:, :half], from_left), right[:, half:]], axis=1)
    left = jnp.concatenate([left[:, :half], add(left[:, half:], from_right)], axis=1)
    return own, along_y(right, 1), along_y(left, -1)


def on_device(
    span_q,
    prompt_kv,
    span_kv,
    decode_q,
    decode_cache,
    decode_new,
    decode_len,
    residual,
    norm_gain,
    router,
    expert_ids,
    capacity,
    w_gate,
    w_up,
    w_down,
):
    here = lax.axis_index("ctx")
    y, z, core = here // 4, (here // 2) % 2, here % 2
    kv = jnp.concatenate([prompt_kv, span_kv], axis=1)
    kv_core = across_core(kv)
    kv_z = across_z(kv)
    q_left, q_right, q_far = along_y(span_q, 1), along_y(span_q, -1), along_y(span_q, 2)
    kv_zc = across_core(kv_z)
    near = (kv, kv_core, ctx_index(0, z, core), ctx_index(0, z, 1 - core))
    other = (kv_z, kv_zc, ctx_index(0, 1 - z, core), ctx_index(0, 1 - z, 1 - core))

    def place_of(steps, blocks):
        source = ctx_index((y + steps) % N_Y, z, core)
        return jnp.stack([source, y * 4 + blocks[2], y * 4 + blocks[3]]).astype(jnp.int32)

    queries = {0: span_q, -1: q_left, 1: q_right, 2: q_far}
    state = {}
    for steps in (0, -1, 1, 2):
        state[steps] = flash_start(place_of(steps, near), queries[steps], near[0], near[1])
    msg = {}
    for steps in (2, -1, 1, 0):
        msg[steps] = flash_end(
            place_of(steps, other), queries[steps], other[0], other[1], state[steps]
        )
    msg_far = along_y(msg[2], 2)
    msg_left = along_y(msg[1], 1)
    msg_right = along_y(msg[-1], -1)

    gate_own, up_own, down_own, kv_zc = lax.optimization_barrier((w_gate, w_up, w_down, kv_zc))
    gate_other = across_core(gate_own)
    up_other = across_core(up_own)
    down_other = across_core(down_own)

    expert_range = jnp.arange(EXPERTS, dtype=jnp.int32)
    flat_ids = expert_ids.reshape(ROWS_DEV * TOPK)
    assign = (flat_ids[:, None] == expert_range[None, :]).astype(jnp.int32)
    prior = jnp.cumsum(assign, axis=0) - assign
    position = jnp.sum(prior * assign, axis=1)
    limit = jnp.sum(assign * capacity[None, :], axis=1)
    slot = jnp.where(position < limit, flat_ids * CAP + position, -1).reshape(ROWS_DEV, TOPK)
    slot_range = jnp.arange(SLOTS, dtype=jnp.int32)[:, None]
    placing = ((slot[:, 0][None, :] == slot_range) | (slot[:, 1][None, :] == slot_range)).astype(
        BF16
    )
    own_placing = lax.dynamic_slice_in_dim(placing, lax.axis_index("exp") * CAP, CAP, 0)

    decode_out = decode_block(decode_q, decode_cache, decode_new, decode_len)
    carried, outgoing = pl.pallas_call(
        dispatch_kernel,
        out_shape=(
            jax.ShapeDtypeStruct((ROWS_DEV, WIDTH), F32),
            jax.ShapeDtypeStruct((EXPERTS, CAP + EXTRA, WIDTH), BF16),
        ),
        in_specs=[VMEM] * 9,
        out_specs=(VMEM, VMEM),
        name="dispatch",
    )(
        msg[0],
        msg_far,
        msg_left,
        msg_right,
        decode_out,
        residual,
        norm_gain.reshape(1, WIDTH),
        router.T,
        placing,
    )
    got = lax.all_to_all(outgoing, "exp", split_axis=0, concat_axis=0, tiled=True)
    first, second, logits = pl.pallas_call(
        arrive_kernel,
        out_shape=(
            jax.ShapeDtypeStruct((CAP, F1), BF16),
            jax.ShapeDtypeStruct((CAP, F2), BF16),
            jax.ShapeDtypeStruct((EXPERTS, ROWS_DEV), F32),
        ),
        in_specs=[VMEM, VMEM],
        out_specs=(VMEM,) * 3,
        name="arrive",
    )(got, own_placing)

    first_z = across_z(first)
    second_left, second_right = along_y(second, 1), along_y(second, -1)
    second_z = across_z(second)
    pair = jnp.concatenate([first, first_z], axis=0)
    pair_left, pair_right = along_y(pair, 1), along_y(pair, -1)
    second_far_a = along_y(second_left[:, : F2 // 2], 1)
    second_far_b = along_y(second_right[:, F2 // 2 :], -1)
    second_left_z = across_z(second_left)
    second_right_z = across_z(second_right)
    pair_far_a = along_y(pair_left[:, : F1 // 2], 1)
    pair_far_b = along_y(pair_right[:, F1 // 2 :], -1)
    second_far_az = across_z(second_far_a)
    second_far_bz = across_z(second_far_b)

    weights = (gate_own, gate_other, up_own, up_other)
    partial = gate_call(
        gate_first,
        (pair, pair_left, pair_right, pair_far_a, pair_far_b),
        ((0, 0), (80, 0), (160, 0), (240, 0), (240, F1 // 2)),
        (),
        weights,
        0,
        F1,
        2,
        F32,
    )
    (hidden,) = gate_call(
        gate_last,
        (
            second,
            second_z,
            second_left,
            second_left_z,
            second_right,
            second_right_z,
            second_far_a,
            second_far_b,
            second_far_az,
            second_far_bz,
        ),
        (
            (0, 0),
            (40, 0),
            (80, 0),
            (120, 0),
            (160, 0),
            (200, 0),
            (240, 0),
            (240, F2 // 2),
            (280, 0),
            (280, F2 // 2),
        ),
        partial,
        weights,
        F1 // F2,
        F2,
        1,
        BF16,
    )

    part_two = down_call(hidden, down_own, down_other, F1, F2, 1024)
    part_one = down_call(hidden, down_own, down_other, 0, F1, 1024)
    two = part_two.reshape(N_Y, 2, CAP, F2)
    two_z = across_z(two[:, 1])
    one = [part_one[80 * i : 80 * i + 80] for i in range(N_Y)]
    one = add(*scatter_y(*one))
    two = add(two[:, 0], two_z)
    two = add(*scatter_y(two[0], two[1], two[2], two[3]))
    one = add(one[:CAP], across_z(one[CAP:]))
    result = jnp.concatenate([one, two], axis=1)
    result = result.reshape(CAP, EXPERTS, WIDTH).transpose(1, 0, 2)
    returned = lax.all_to_all(result, "exp", split_axis=0, concat_axis=0, tiled=True)

    onehot = expert_ids[:, :, None] == expert_range[None, None, :]
    chosen = jnp.sum(jnp.where(onehot, logits.T[:, None, :], 0.0), axis=-1)
    route_weight = jax.nn.sigmoid(chosen - chosen[:, ::-1])
    mix_shape = jax.ShapeDtypeStruct((ROWS_DEV, SLOTS), BF16)
    mix_hi, mix_lo = pl.pallas_call(
        mixing_kernel,
        out_shape=(mix_shape, mix_shape),
        in_specs=[VMEM, VMEM],
        out_specs=(VMEM, VMEM),
        name="mixing",
    )(slot, route_weight)
    return pl.pallas_call(
        final_kernel,
        out_shape=jax.ShapeDtypeStruct((ROWS_DEV, WIDTH), BF16),
        in_specs=[VMEM] * 4,
        out_specs=VMEM,
        name="final",
    )(mix_hi, mix_lo, returned.reshape(SLOTS, WIDTH), carried)


def solution(mesh):
    placed = (
        P("ctx", "exp"),
        P(None, "ctx", "exp"),
        P(None, "ctx", "exp"),
        P("ctx", "exp"),
        P(None, "ctx", None, "exp"),
        P(None, "ctx", "exp"),
        P("ctx"),
        P("ctx", "exp"),
        P("exp"),
        P("exp", None),
        P("ctx", None),
        P(),
        P("exp", None, "ctx"),
        P("exp", None, "ctx"),
        P("exp", "ctx", None),
    )
    return jax.shard_map(
        on_device, mesh=mesh, in_specs=placed, out_specs=P("ctx", "exp"), check_vma=False
    )
```

time: 550 us -> 237 us (0.43)
  waiting for transfers between devices: 287 us -> 84.9 us
  Pallas kernels: 0 us -> 62.5 us
  other arithmetic: 65 us -> 5.75 us
  matrix products: 53.6 us -> 3.39 us
  blocking collectives: 43 us -> 0 us
  local copies, waits for them, and re-layouts: 28.2 us -> 11.9 us
  between operations: 13.8 us -> 0.86 us
  starting transfers between devices: 56.7 us -> 62.5 us
    reduce_scatter x1 -> x0, waiting for transfers between devices: 94.7 us -> none  [on_device(): lax.psum_scatter(jnp.einsum('ref,efd->red', hidden, w_down, preferred_ele...]
    all_gather x1 -> x0, waiting for transfers between devices: 68.9 us -> none  [on_device(): piece = lax.all_gather(arrived, 'ctx', axis=0, tiled=True)]
    pallas_call x0 -> x16, Pallas kernels: none -> 62.5 us  [the longest x2 17.7 us: gate_call(): pl.pallas_call(functools.partial(kernel, layout, len(pieces)), grid=(2 *...]
    ppermute x64 -> x36, waiting for transfers between devices: 123 us -> 72.2 us  [moved(): return lax.ppermute(value, 'ctx', pairs)]
    dot_general x41 -> x3, matrix products: 53.6 us -> 3.39 us  [the longest x1 1.7 us: decode_block(): jnp.einsum('rqd,rld->rql', queries, keys, preferred_element_type=F32)]
    unnamed x2 -> x1, other arithmetic: 34.4 us -> 0.01 us
    all_to_all x2 -> x0, blocking collectives: 23.3 us -> none  [the longest x1 12.6 us: on_device(): lax.all_to_all(result, 'exp', split_axis=2, concat_axis=1, tiled=True)]
    psum x1 -> x0, blocking collectives: 19.8 us -> none  [on_device(): squares, logits = lax.psum((squares, partial_logits), 'exp')]
  transfers between devices with their start and end apart: 66 -> 38, of which waited for: 34 -> 19; matrix products, arithmetic and copies ran while one was open for 9% -> 6% of each run, Pallas kernels for 0% -> 24%
where the time goes in v1:
time: 237 us; the launch traced here: 232 us
  waiting for transfers between devices  84.9 us (36%)
  starting transfers between devices  62.5 us (26%)
  Pallas kernels  62.5 us (26%)
  local copies, waits for them, and re-layouts  11.9 us (5%)
  other arithmetic  5.75 us (2%)
  matrix products  3.39 us (1%)
    ppermute x36, waiting for transfers between devices, moved(): return lax.ppermute(value, 'ctx', pairs)  72.2 us
    ppermute x36, starting transfers between devices, moved(): return lax.ppermute(value, 'ctx', pairs)  52.7 us
    pallas_call x2, Pallas kernels, gate_call(): pl.pallas_call(functools.partial(kernel, layout, len(pieces)), grid=(2 *...  17.7 us
    pallas_call x4, Pallas kernels, flash_end(): pl.pallas_call(flash_last, out_shape=jax.ShapeDtypeStruct((SPAN_DEV, MSG)...  13.2 us
    pallas_call x4, Pallas kernels, flash_start(): pl.pallas_call(flash_first, out_shape=(shape,) * 3, in_specs=[SMEM, VMEM,...  12.9 us
    pallas_call x2, Pallas kernels, down_call(): pl.pallas_call(down_kernel, grid=(count,), out_shape=jax.ShapeDtypeStruct...  8.46 us
    all_to_all x1, waiting for transfers between devices, on_device(): lax.all_to_all(outgoing, 'exp', split_axis=0, concat_axis=0, tiled=True)  7.64 us
    unnamed x34, local copies, waits for them, and re-layouts  5.89 us
  transfers between devices with their start and end apart: 38, of which 19 were waited for; matrix products, arithmetic and copies ran while one was open for 6% of the time, Pallas kernels for 24%

profile of v1, /device:TPU:0, one launch (start us, length us, event | category | flops | bytes accessed | tf_op | source)
XLA Modules:
  0.0 231.9 jit_solution(15121045290451877317)
XLA Ops:
  2.0 4.0 %collective-permute-start = (bf16[2,1152,128]{2,1,0:T(8,128)(2,1)S(1)}, bf16[2,1152,128]{2,1,0:T(8,128)(2,1)S(1)}, u32[]{:S(2)}, u32[]{:S(2)}) collective-permute-start(bf16[2,1152,128]{2,1,0:T(8,128)(2,1)S(1)} %constant_dynamic-update-slice_fusion.a_ref), channel_id=1, source_target_pairs={{0,16},{8,24},{16,0},{24,8},{32,48},{40,56},{48,32},{56,40},{64,80... | collective-permute-start | bytes 1769480 | tf_op jit(solution)/shard_map/ppermute | solution.py:49
  8.3 11.0 %collective-permute-done.a_ref = bf16[2,1152,128]{2,1,0:T(8,128)(2,1)S(1)} collective-permute-done((bf16[2,1152,128]{2,1,0:T(8,128)(2,1)S(1)}, bf16[2,1152,128]{2,1,0:T(8,128)(2,1)S(1)}, u32[]{:S(2)}, u32[]{:S(2)}) %collective-permute-start) | collective-permute-done | bytes 589856 | tf_op jit(solution)/shard_map/ppermute | solution.py:49
  37.7 4.2 %collective-permute-done.5.q_ref = bf16[128,768]{1,0:T(8,128)(2,1)S(1)} collective-permute-done((bf16[128,768]{1,0:T(8,128)(2,1)S(1)}, bf16[128,768]{1,0:T(8,128)(2,1)S(1)}, u32[]{:S(2)}, u32[]{:S(2)}) %collective-permute-start.5) | collective-permute-done | bytes 196640 | tf_op jit(solution)/shard_map/ppermute | solution.py:49
  48.4 3.9 %collective-permute-start.8 = (bf16[128,896]{1,0:T(8,128)(2,1)S(1)}, bf16[128,896]{1,0:T(8,128)(2,1)S(1)}, u32[]{:S(2)}, u32[]{:S(2)}) collective-permute-start(bf16[128,896]{1,0:T(8,128)(2,1)S(1)} %flash_last.7), channel_id=1, source_target_pairs={{0,96},{8,104},{16,112},{24,120},{32,0},{40,8},{48,16},{56,24},{64... | collective-permute-start | bytes 688136 | tf_op jit(solution)/shard_map/ppermute | solution.py:49
  72.4 4.2 %dispatch.1 = (f32[144,768]{1,0:T(8,128)}, bf16[8,48,768]{2,1,0:T(8,128)(2,1)}) custom-call(bf16[128,896]{1,0:T(8,128)(2,1)} %copy-done, bf16[128,896]{1,0:T(8,128)(2,1)} %copy-done.8, bf16[128,896]{1,0:T(8,128)(2,1)} %copy-done.7, bf16[128,896]{1,0:T(8,128)(2,1)} %copy-done.6, bf16[16,768]{1,0:T(8,128)(2,1)} %bitcast.76, bf16[144,768]{1,0:T(8,128)(2,1)} %residual_ref.1, ...), custom_call_target="tpu_custom_call" | custom-call | tf_op jit(solution)/shard_map/dispatch/pallas_call | solution.py:450
  76.5 5.0 %all-to-all-start = ((bf16[8,48,768]{2,1,0:T(8,128)(2,1)}), bf16[8,48,768]{2,1,0:T(8,128)(2,1)S(1)}, u32[]{:S(2)}, u32[]{:S(2)}) async-start(bf16[8,48,768]{2,1,0:T(8,128)(2,1)} %get-tuple-element.41), calls=%async_computation | async-start | bytes 1179648 | tf_op jit(solution)/shard_map/all_to_all | solution.py:470
  82.9 7.6 %all-to-all-done.got_ref = bf16[8,48,768]{2,1,0:T(8,128)(2,1)S(1)} async-done(((bf16[8,48,768]{2,1,0:T(8,128)(2,1)}), bf16[8,48,768]{2,1,0:T(8,128)(2,1)S(1)}, u32[]{:S(2)}, u32[]{:S(2)}) %all-to-all-start) | async-done | bytes 589856 | tf_op jit(solution)/shard_map/all_to_all | solution.py:470
  93.4 3.6 %collective-permute-start.18 = (bf16[40,4096]{1,0:T(8,128)(2,1)}, bf16[40,4096]{1,0:T(8,128)(2,1)S(1)}, u32[]{:S(2)}, u32[]{:S(2)}) collective-permute-start(bf16[40,4096]{1,0:T(8,128)(2,1)} %get-tuple-element.46), channel_id=1, source_target_pairs={{0,16},{8,24},{16,0},{24,8},{32,48},{40,56},{48,32},{56,40},{64,80... | collective-permute-start | bytes 983048 | tf_op jit(solution)/shard_map/ppermute | solution.py:49
  100.3 3.4 %collective-permute-done.10.refs_2_ = bf16[40,2048]{1,0:T(8,128)(2,1)S(1)} collective-permute-done((bf16[40,2048]{1,0:T(8,128)(2,1)}, bf16[40,2048]{1,0:T(8,128)(2,1)S(1)}, u32[]{:S(2)}, u32[]{:S(2)}) %collective-permute-start.10) | collective-permute-done | bytes 163872 | tf_op jit(solution)/shard_map/ppermute | solution.py:49
  105.8 4.9 %collective-permute-done.12.refs_4_ = bf16[40,2048]{1,0:T(8,128)(2,1)S(1)} collective-permute-done((bf16[40,2048]{1,0:T(8,128)(2,1)}, bf16[40,2048]{1,0:T(8,128)(2,1)S(1)}, u32[]{:S(2)}, u32[]{:S(2)}) %collective-permute-start.12) | collective-permute-done | bytes 163872 | tf_op jit(solution)/shard_map/ppermute | solution.py:49
  114.0 9.4 %collective-permute-done.19.refs_1_ = bf16[80,4096]{1,0:T(8,128)(2,1)S(1)} collective-permute-done((bf16[80,4096]{1,0:T(8,128)(2,1)S(1)}, bf16[80,4096]{1,0:T(8,128)(2,1)S(1)}, u32[]{:S(2)}, u32[]{:S(2)}) %collective-permute-start.19) | collective-permute-done | bytes 655392 | tf_op jit(solution)/shard_map/ppermute | solution.py:49
  132.3 5.0 %collective-permute-done.21.refs_3_ = bf16[80,2048]{1,0:T(8,128)(2,1)S(1)} collective-permute-done((bf16[80,2048]{1,0:T(8,128)(2,1)S(1)}, bf16[80,2048]{1,0:T(8,128)(2,1)S(1)}, u32[]{:S(2)}, u32[]{:S(2)}) %collective-permute-start.21) | collective-permute-done | bytes 327712 | tf_op jit(solution)/shard_map/ppermute | solution.py:49
  141.1 3.5 %collective-permute-start.17 = (bf16[40,1024]{1,0:T(8,128)(2,1)S(1)}, bf16[40,1024]{1,0:T(8,128)(2,1)S(1)}, u32[]{:S(2)}, u32[]{:S(2)}) collective-permute-start(bf16[40,1024]{1,0:T(8,128)(2,1)S(1)} %collective-permute-done.15.refs_7_), channel_id=1, source_target_pairs={{0,16},{8,24},{16,0},{24,8},{32,48},{40,56},{48,32},{56,40},{64,80... | collective-permute-start | bytes 245768 | tf_op jit(solution)/shard_map/ppermute | solution.py:49
  144.6 10.8 %gate_first.1 = (f32[320,1024]{1,0:T(8,128)S(1)}, f32[320,1024]{1,0:T(8,128)S(1)}) custom-call(bf16[80,4096]{1,0:T(8,128)(2,1)S(1)} %constant_dynamic-update-slice_fusion.2.refs_0_, bf16[80,4096]{1,0:T(8,128)(2,1)S(1)} %collective-permute-done.19.refs_1_, bf16[80,4096]{1,0:T(8,128)(2,1)S(1)} %collective-permute-done.20.refs_2_, ...), custom_call_target="tpu_custom_call" | custom-call | flops 5368709120 | bytes 16777216 | tf_op jit(solution)/shard_map/gate_first/pallas_call | solution.py:292
  155.5 6.9 %gate_last.1.hidden_ref = bf16[320,1024]{1,0:T(8,128)(2,1)S(1)} custom-call(bf16[40,2048]{1,0:T(8,128)(2,1)S(1)} %copy-done.1, bf16[40,2048]{1,0:T(8,128)(2,1)S(1)} %collective-permute-done.9.refs_1_, bf16[40,2048]{1,0:T(8,128)(2,1)S(1)} %collective-permute-done.10.refs_2_, bf16[40,2048]{1,0:T(8,128)(2,1)S(1)} %collective-permute-done.11.refs_3_, ...), custom_call_target="tpu_custom_call" | custom-call | flops 2684354560 | bytes 8388608 | tf_op jit(solution)/shard_map/gate_last/pallas_call | solution.py:292
  162.5 5.4 %down.2 = bf16[320,4096]{1,0:T(8,128)(2,1)S(1)} custom-call(bf16[320,1024]{1,0:T(8,128)(2,1)S(1)} %gate_last.1.hidden_ref, bf16[1,512,6144]{2,1,0:T(8,128)(2,1)S(1)} %bitcast.71, bf16[1,512,6144]{2,1,0:T(8,128)(2,1)} %collective-permute-done.25.other_ref), custom_call_target="tpu_custom_call" | custom-call | flops 2684354560 | bytes 8388608 | tf_op jit(solution)/shard_map/down/pallas_call | solution.py:319
  174.8 5.1 %collective-permute-done.26 = bf16[80,2048]{1,0:T(8,128)(2,1)S(1)} collective-permute-done((bf16[80,2048]{1,0:T(8,128)(2,1)S(1)}, bf16[80,2048]{1,0:T(8,128)(2,1)S(1)}, u32[]{:S(2)}, u32[]{:S(2)}) %collective-permute-start.26) | collective-permute-done | bytes 327712 | tf_op jit(solution)/shard_map/ppermute | solution.py:49
  180.3 6.3 %collective-permute-done.31 = bf16[4,40,2048]{2,1,0:T(8,128)(2,1)S(1)} collective-permute-done((bf16[4,40,2048]{2,1,0:T(8,128)(2,1)S(1)}, bf16[4,40,2048]{2,1,0:T(8,128)(2,1)S(1)}, u32[]{:S(2)}, u32[]{:S(2)}) %collective-permute-start.31) | collective-permute-done | bytes 655392 | tf_op jit(solution)/shard_map/ppermute | solution.py:49
  190.4 4.3 %collective-permute-done.32 = bf16[40,1024]{1,0:T(8,128)(2,1)S(1)} collective-permute-done((bf16[40,1024]{1,0:T(8,128)(2,1)S(1)}, bf16[40,1024]{1,0:T(8,128)(2,1)S(1)}, u32[]{:S(2)}, u32[]{:S(2)}) %collective-permute-start.32) | collective-permute-done | bytes 81952 | tf_op jit(solution)/shard_map/ppermute | solution.py:49
  194.8 5.2 %collective-permute-done.34 = bf16[40,1024]{1,0:T(8,128)(2,1)S(1)} collective-permute-done((bf16[40,1024]{1,0:T(8,128)(2,1)S(1)}, bf16[40,1024]{1,0:T(8,128)(2,1)S(1)}, u32[]{:S(2)}, u32[]{:S(2)}) %collective-permute-start.34) | collective-permute-done | bytes 81952 | tf_op jit(solution)/shard_map/ppermute | solution.py:49
  200.1 3.8 %collective-permute-start.35 = (bf16[40,2048]{1,0:T(8,128)(2,1)S(1)}, bf16[40,2048]{1,0:T(8,128)(2,1)S(1)}, u32[]{:S(2)}, u32[]{:S(2)}) collective-permute-start(bf16[40,2048]{1,0:T(8,128)(2,1)S(1)} %pad_maximum_fusion.4), channel_id=1, source_target_pairs={{0,96},{8,104},{16,112},{24,120},{32,0},{40,8},{48,16},{56,24},{64... | collective-permute-start | bytes 491528 | tf_op jit(solution)/shard_map/ppermute | solution.py:49
  206.8 8.1 %collective-permute-done.30 = bf16[40,4096]{1,0:T(8,128)(2,1)S(1)} collective-permute-done((bf16[40,4096]{1,0:T(8,128)(2,1)S(1)}, bf16[40,4096]{1,0:T(8,128)(2,1)S(1)}, u32[]{:S(2)}, u32[]{:S(2)}) %collective-permute-start.30) | collective-permute-done | bytes 327712 | tf_op jit(solution)/shard_map/ppermute | solution.py:49
  215.8 4.8 %all-to-all-start.1 = ((bf16[8,40,768]{2,1,0:T(8,128)(2,1)}), bf16[8,40,768]{2,1,0:T(8,128)(2,1)S(1)}, u32[]{:S(2)}, u32[]{:S(2)}) async-start(bf16[8,40,768]{2,1,0:T(8,128)(2,1)} %bitcast.67), calls=%async_computation.1 | async-start | bytes 983040 | tf_op jit(solution)/shard_map/all_to_all | solution.py:554
  223.5 5.1 %all-to-all-done.1 = bf16[8,40,768]{2,1,0:T(8,128)(2,1)S(1)} async-done(((bf16[8,40,768]{2,1,0:T(8,128)(2,1)}), bf16[8,40,768]{2,1,0:T(8,128)(2,1)S(1)}, u32[]{:S(2)}, u32[]{:S(2)}) %all-to-all-start.1) | async-done | bytes 491552 | tf_op jit(solution)/shard_map/all_to_all | solution.py:554
  (168 shorter events, 95.4 us)
Async XLA Ops:
  2.0 17.4 %collective-permute-start = (bf16[2,1152,128]{2,1,0:T(8,128)(2,1)S(1)}, bf16[2,1152,128]{2,1,0:T(8,128)(2,1)S(1)}, u32[]{:S(2)}, u32[]{:S(2)}) collective-permute-start(bf16[2,1152,128]{2,1,0:T(8,128)(2,1)S(1)} %constant_dynamic-update-slice_fusion.a_ref), channel_id=1, source_target_pairs={{0,16},{8,24},{16,0},{24,8},{32,48},{40,56},{48,32},{56,40},{64,80... | collective-permute-start | bytes 1769480 | tf_op jit(solution)/shard_map/ppermute | solution.py:49
  6.0 27.3 %collective-permute-start.2 = (bf16[2,1152,128]{2,1,0:T(8,128)(2,1)S(1)}, bf16[2,1152,128]{2,1,0:T(8,128)(2,1)S(1)}, u32[]{:S(2)}, u32[]{:S(2)}) collective-permute-start(bf16[2,1152,128]{2,1,0:T(8,128)(2,1)S(1)} %constant_dynamic-update-slice_fusion.a_ref), channel_id=1, source_target_pairs={{0,8},{8,0},{16,24},{24,16},{32,40},{40,32},{48,56},{56,48},{64,72... | collective-permute-start | bytes 1769480 | tf_op jit(solution)/shard_map/ppermute | solution.py:49
  6.0 24.2 %collective-permute-start.7 = (bf16[128,768]{1,0:T(8,128)(2,1)}, bf16[128,768]{1,0:T(8,128)(2,1)S(1)}, u32[]{:S(2)}, u32[]{:S(2)}) collective-permute-start(bf16[128,768]{1,0:T(8,128)(2,1)} %q_ref.3), channel_id=1, source_target_pairs={{0,32},{8,40},{16,48},{24,56},{32,64},{40,72},{48,80},{56,88},{64,... | collective-permute-start | bytes 589832 | tf_op jit(solution)/shard_map/ppermute | solution.py:49
  22.7 118.2 %collective-permute-start.23 = (bf16[1,6144,512]{2,1,0:T(8,128)(2,1)}, bf16[1,6144,512]{2,1,0:T(8,128)(2,1)}, u32[]{:S(2)}, u32[]{:S(2)}) collective-permute-start(bf16[1,6144,512]{2,1,0:T(8,128)(2,1)} %refs_12_), channel_id=1, source_target_pairs={{0,8},{8,0},{16,24},{24,16},{32,40},{40,32},{48,56},{56,48},{64,72... | collective-permute-start | bytes 18874376 | tf_op jit(solution)/shard_map/ppermute | solution.py:49
  23.2 117.9 %collective-permute-start.24 = (bf16[1,6144,512]{2,1,0:T(8,128)(2,1)}, bf16[1,6144,512]{2,1,0:T(8,128)(2,1)}, u32[]{:S(2)}, u32[]{:S(2)}) collective-permute-start(bf16[1,6144,512]{2,1,0:T(8,128)(2,1)} %refs_14_), channel_id=1, source_target_pairs={{0,8},{8,0},{16,24},{24,16},{32,40},{40,32},{48,56},{56,48},{64,72... | collective-permute-start | bytes 18874376 | tf_op jit(solution)/shard_map/ppermute | solution.py:49
  24.7 137.7 %collective-permute-start.25 = (bf16[1,512,6144]{2,1,0:T(8,128)(2,1)}, bf16[1,512,6144]{2,1,0:T(8,128)(2,1)}, u32[]{:S(2)}, u32[]{:S(2)}) collective-permute-start(bf16[1,512,6144]{2,1,0:T(8,128)(2,1)} %own_ref.1), channel_id=1, source_target_pairs={{0,8},{8,0},{16,24},{24,16},{32,40},{40,32},{48,56},{56,48},{64,72... | collective-permute-start | bytes 18874376 | tf_op jit(solution)/shard_map/ppermute | solution.py:49
  30.2 11.7 %collective-permute-start.5 = (bf16[128,768]{1,0:T(8,128)(2,1)S(1)}, bf16[128,768]{1,0:T(8,128)(2,1)S(1)}, u32[]{:S(2)}, u32[]{:S(2)}) collective-permute-start(bf16[128,768]{1,0:T(8,128)(2,1)S(1)} %copy-done.2), channel_id=1, source_target_pairs={{0,96},{8,104},{16,112},{24,120},{32,0},{40,8},{48,16},{56,24},{64... | collective-permute-start | bytes 589832 | tf_op jit(solution)/shard_map/ppermute | solution.py:49
  33.3 19.0 %collective-permute-start.3 = (bf16[128,768]{1,0:T(8,128)(2,1)S(1)}, bf16[128,768]{1,0:T(8,128)(2,1)S(1)}, u32[]{:S(2)}, u32[]{:S(2)}) collective-permute-start(bf16[128,768]{1,0:T(8,128)(2,1)S(1)} %copy-done.2), channel_id=1, source_target_pairs={{0,64},{8,72},{16,80},{24,88},{32,96},{40,104},{48,112},{56,120},{... | collective-permute-start | bytes 589832 | tf_op jit(solution)/shard_map/ppermute | solution.py:49
  48.4 13.9 %collective-permute-start.8 = (bf16[128,896]{1,0:T(8,128)(2,1)S(1)}, bf16[128,896]{1,0:T(8,128)(2,1)S(1)}, u32[]{:S(2)}, u32[]{:S(2)}) collective-permute-start(bf16[128,896]{1,0:T(8,128)(2,1)S(1)} %flash_last.7), channel_id=1, source_target_pairs={{0,96},{8,104},{16,112},{24,120},{32,0},{40,8},{48,16},{56,24},{64... | collective-permute-start | bytes 688136 | tf_op jit(solution)/shard_map/ppermute | solution.py:49
  58.9 12.7 %collective-permute-start.6 = (bf16[128,896]{1,0:T(8,128)(2,1)S(1)}, bf16[128,896]{1,0:T(8,128)(2,1)S(1)}, u32[]{:S(2)}, u32[]{:S(2)}) collective-permute-start(bf16[128,896]{1,0:T(8,128)(2,1)S(1)} %flash_last.6), channel_id=1, source_target_pairs={{0,32},{8,40},{16,48},{24,56},{32,64},{40,72},{48,80},{56,88},{64,... | collective-permute-start | bytes 688136 | tf_op jit(solution)/shard_map/ppermute | solution.py:49
  76.5 14.0 %all-to-all-start = ((bf16[8,48,768]{2,1,0:T(8,128)(2,1)}), bf16[8,48,768]{2,1,0:T(8,128)(2,1)S(1)}, u32[]{:S(2)}, u32[]{:S(2)}) async-start(bf16[8,48,768]{2,1,0:T(8,128)(2,1)} %get-tuple-element.41), calls=%async_computation | async-start | bytes 1179648 | tf_op jit(solution)/shard_map/all_to_all | solution.py:470
  93.4 10.9 %collective-permute-start.18 = (bf16[40,4096]{1,0:T(8,128)(2,1)}, bf16[40,4096]{1,0:T(8,128)(2,1)S(1)}, u32[]{:S(2)}, u32[]{:S(2)}) collective-permute-start(bf16[40,4096]{1,0:T(8,128)(2,1)} %get-tuple-element.46), channel_id=1, source_target_pairs={{0,16},{8,24},{16,0},{24,8},{32,48},{40,56},{48,32},{56,40},{64,80... | collective-permute-start | bytes 983048 | tf_op jit(solution)/shard_map/ppermute | solution.py:49
  110.7 12.7 %collective-permute-start.19 = (bf16[80,4096]{1,0:T(8,128)(2,1)S(1)}, bf16[80,4096]{1,0:T(8,128)(2,1)S(1)}, u32[]{:S(2)}, u32[]{:S(2)}) collective-permute-start(bf16[80,4096]{1,0:T(8,128)(2,1)S(1)} %constant_dynamic-update-slice_fusion.2.refs_0_), channel_id=1, source_target_pairs={{0,32},{8,40},{16,48},{24,56},{32,64},{40,72},{48,80},{56,88},{64,... | collective-permute-start | bytes 1966088 | tf_op jit(solution)/shard_map/ppermute | solution.py:49
  111.3 12.9 %collective-permute-start.20 = (bf16[80,4096]{1,0:T(8,128)(2,1)S(1)}, bf16[80,4096]{1,0:T(8,128)(2,1)S(1)}, u32[]{:S(2)}, u32[]{:S(2)}) collective-permute-start(bf16[80,4096]{1,0:T(8,128)(2,1)S(1)} %constant_dynamic-update-slice_fusion.2.refs_0_), channel_id=1, source_target_pairs={{0,96},{8,104},{16,112},{24,120},{32,0},{40,8},{48,16},{56,24},{64... | collective-permute-start | bytes 1966088 | tf_op jit(solution)/shard_map/ppermute | solution.py:49
  137.3 18.1 %collective-permute-start.11 = (bf16[40,2048]{1,0:T(8,128)(2,1)S(1)}, bf16[40,2048]{1,0:T(8,128)(2,1)S(1)}, u32[]{:S(2)}, u32[]{:S(2)}) collective-permute-start(bf16[40,2048]{1,0:T(8,128)(2,1)S(1)} %collective-permute-done.10.refs_2_), channel_id=1, source_target_pairs={{0,16},{8,24},{16,0},{24,8},{32,48},{40,56},{48,32},{56,40},{64,80... | collective-permute-start | bytes 491528 | tf_op jit(solution)/shard_map/ppermute | solution.py:49
  137.6 17.9 %collective-permute-start.13 = (bf16[40,2048]{1,0:T(8,128)(2,1)S(1)}, bf16[40,2048]{1,0:T(8,128)(2,1)S(1)}, u32[]{:S(2)}, u32[]{:S(2)}) collective-permute-start(bf16[40,2048]{1,0:T(8,128)(2,1)S(1)} %collective-permute-done.12.refs_4_), channel_id=1, source_target_pairs={{0,16},{8,24},{16,0},{24,8},{32,48},{40,56},{48,32},{56,40},{64,80... | collective-permute-start | bytes 491528 | tf_op jit(solution)/shard_map/ppermute | solution.py:49
  140.8 14.6 %collective-permute-start.16 = (bf16[40,1024]{1,0:T(8,128)(2,1)S(1)}, bf16[40,1024]{1,0:T(8,128)(2,1)S(1)}, u32[]{:S(2)}, u32[]{:S(2)}) collective-permute-start(bf16[40,1024]{1,0:T(8,128)(2,1)S(1)} %collective-permute-done.14.refs_6_), channel_id=1, source_target_pairs={{0,16},{8,24},{16,0},{24,8},{32,48},{40,56},{48,32},{56,40},{64,80... | collective-permute-start | bytes 245768 | tf_op jit(solution)/shard_map/ppermute | solution.py:49
  141.1 14.3 %collective-permute-start.17 = (bf16[40,1024]{1,0:T(8,128)(2,1)S(1)}, bf16[40,1024]{1,0:T(8,128)(2,1)S(1)}, u32[]{:S(2)}, u32[]{:S(2)}) collective-permute-start(bf16[40,1024]{1,0:T(8,128)(2,1)S(1)} %collective-permute-done.15.refs_7_), channel_id=1, source_target_pairs={{0,16},{8,24},{16,0},{24,8},{32,48},{40,56},{48,32},{56,40},{64,80... | collective-permute-start | bytes 245768 | tf_op jit(solution)/shard_map/ppermute | solution.py:49
  168.0 11.9 %collective-permute-start.26 = (bf16[80,2048]{1,0:T(8,128)(2,1)S(1)}, bf16[80,2048]{1,0:T(8,128)(2,1)S(1)}, u32[]{:S(2)}, u32[]{:S(2)}) collective-permute-start(bf16[80,2048]{1,0:T(8,128)(2,1)S(1)} %get-tuple-element.59), channel_id=1, source_target_pairs={{0,32},{8,40},{16,48},{24,56},{32,64},{40,72},{48,80},{56,88},{64,... | collective-permute-start | bytes 983048 | tf_op jit(solution)/shard_map/ppermute | solution.py:49
  168.1 11.8 %collective-permute-start.28 = (bf16[80,2048]{1,0:T(8,128)(2,1)S(1)}, bf16[80,2048]{1,0:T(8,128)(2,1)S(1)}, u32[]{:S(2)}, u32[]{:S(2)}) collective-permute-start(bf16[80,2048]{1,0:T(8,128)(2,1)S(1)} %get-tuple-element.60), channel_id=1, source_target_pairs={{0,96},{8,104},{16,112},{24,120},{32,0},{40,8},{48,16},{56,24},{64... | collective-permute-start | bytes 983048 | tf_op jit(solution)/shard_map/ppermute | solution.py:49
  174.5 12.2 %collective-permute-start.31 = (bf16[4,40,2048]{2,1,0:T(8,128)(2,1)S(1)}, bf16[4,40,2048]{2,1,0:T(8,128)(2,1)S(1)}, u32[]{:S(2)}, u32[]{:S(2)}) collective-permute-start(bf16[4,40,2048]{2,1,0:T(8,128)(2,1)S(1)} %slice_bitcast_fusion), channel_id=1, source_target_pairs={{0,16},{8,24},{16,0},{24,8},{32,48},{40,56},{48,32},{56,40},{64,80... | collective-permute-start | bytes 1966088 | tf_op jit(solution)/shard_map/ppermute | solution.py:49
  180.2 23.7 %collective-permute-start.27 = (bf16[80,4096]{1,0:T(8,128)(2,1)S(1)}, bf16[80,4096]{1,0:T(8,128)(2,1)S(1)}, u32[]{:S(2)}, u32[]{:S(2)}) collective-permute-start(bf16[80,4096]{1,0:T(8,128)(2,1)S(1)} %pad_maximum_fusion), channel_id=1, source_target_pairs={{0,32},{8,40},{16,48},{24,56},{32,64},{40,72},{48,80},{56,88},{64,... | collective-permute-start | bytes 1966088 | tf_op jit(solution)/shard_map/ppermute | solution.py:49
  187.0 16.8 %collective-permute-start.29 = (bf16[80,4096]{1,0:T(8,128)(2,1)S(1)}, bf16[80,4096]{1,0:T(8,128)(2,1)S(1)}, u32[]{:S(2)}, u32[]{:S(2)}) collective-permute-start(bf16[80,4096]{1,0:T(8,128)(2,1)S(1)} %pad_maximum_fusion.1), channel_id=1, source_target_pairs={{0,96},{8,104},{16,112},{24,120},{32,0},{40,8},{48,16},{56,24},{64... | collective-permute-start | bytes 1966088 | tf_op jit(solution)/shard_map/ppermute | solution.py:49
  215.8 12.8 %all-to-all-start.1 = ((bf16[8,40,768]{2,1,0:T(8,128)(2,1)}), bf16[8,40,768]{2,1,0:T(8,128)(2,1)S(1)}, u32[]{:S(2)}, u32[]{:S(2)}) async-start(bf16[8,40,768]{2,1,0:T(8,128)(2,1)} %bitcast.67), calls=%async_computation.1 | async-start | bytes 983040 | tf_op jit(solution)/shard_map/all_to_all | solution.py:554
  (29 other events, 245.2 us)
